TPU v7x, 32 devices: a whole 2x2x4 slice. The times are simulated.
32 devices in a mesh: hours: 2 (over x), row: 8 (over z, y), col: 2 (over core).
Axes of the slice: x: 2, y: 2, z: 4, core: 2. Of those that a mesh axis runs over, the one named last changes fastest.
Arguments:
- spectra: bfloat16 [24, 2, 64, 4096], P('hours', None, 'row', 'col'), parts along dimension 0, may hold values from -6 to 6
- masks: int32 [24, 64], P('hours', 'row'), parts along dimension 0, may hold values 0 or 1
Outputs:
- correlations: float32 [128, 2, 32, 128], P(('hours', 'row'), 'col'), parts along dimension 0
There are 2 independent parts, one for each index of `hours`. A program takes and returns all parts, laid end to end along the dimension named above; each array names one. Nothing has to cross between parts.
All inputs are finite; a program needn't handle non-finite values. No bound on the sum of `masks` on one device may be relied on, other than what follows from the above.
Results may differ from a plain program's by a relative error of at most 0.0054.
Values may be sent and summed in bfloat16 or wider, within the bound.
A program may use at most 128 MiB of HBM per device.

v0:
```python
import math
import jax
import jax.numpy as jnp
from jax import lax
from jax.sharding import PartitionSpec as P

F = 4096
SMOOTH = 32
LAGS = 128
EPSILON = 1e-05
BLOCK_LIMIT = 64


def with_halo(cells, sides, width):
    for axis, dim in sides:
        count = lax.axis_size(axis)
        ends = count - 1
        head = lax.slice_in_dim(cells, 0, width, axis=dim)
        tail = lax.slice_in_dim(cells, cells.shape[dim] - width, cells.shape[dim], axis=dim)
        cells = jnp.concatenate(
            [
                lax.ppermute(tail, axis, [(i, (i + 1) % count) for i in range(ends)]),
                cells,
                lax.ppermute(head, axis, [((i + 1) % count, i) for i in range(ends)]),
            ],
            axis=dim,
        )
    return cells


def cosine_table(first, count):
    freqs = first + jnp.arange(count, dtype=jnp.int32)
    shifts = jnp.arange(1, LAGS + 1, dtype=jnp.int32)
    phase = freqs[:, None] * shifts[None, :] % (2 * F)
    angle = jnp.pi * phase.astype(jnp.float32) / F
    factor = 1.0 / math.sqrt(F)
    return jnp.concatenate([jnp.cos(angle) * factor, -jnp.sin(angle) * factor], axis=0).astype(
        jnp.bfloat16
    )


def whiten(values, padded, live):
    total = lax.reduce_window(
        padded, jnp.array(0, padded.dtype), lax.add, (1, 1, 2 * SMOOTH + 1), (1, 1, 1), "VALID"
    )
    amplitude = total / (2 * SMOOTH + 1) + EPSILON
    return (values / amplitude[:, None] * live[:, None, :, None]).astype(jnp.bfloat16)


def stack_spectra(own, own_live, other, other_live):
    shape = (own.shape[2], other.shape[2], own.shape[3])
    real = jnp.zeros(shape, jnp.float32)
    imag = jnp.zeros(shape, jnp.float32)
    for window in range(own.shape[0]):
        left_re = own[window, 0].astype(jnp.float32)[:, None, :]
        left_im = own[window, 1].astype(jnp.float32)[:, None, :]
        right_re = other[window, 0].astype(jnp.float32)[None, :, :]
        right_im = other[window, 1].astype(jnp.float32)[None, :, :]
        real = real + (left_re * right_re + left_im * right_im)
        imag = imag + (left_im * right_re - left_re * right_im)
    count = jnp.maximum(jnp.dot(own_live.T, other_live, preferred_element_type=jnp.float32), 1.0)
    return (jnp.stack([real, imag], axis=2) / count[:, :, None, None]).astype(jnp.bfloat16)


def correlate(own, own_live, other, other_live, table):
    stacked = stack_spectra(own, own_live, other, other_live)
    rows = stacked.reshape(stacked.shape[0] * stacked.shape[1], -1)
    result = jnp.dot(rows, table, preferred_element_type=jnp.float32)
    return result.reshape(stacked.shape[0], stacked.shape[1], -1)


def magnitudes(values):
    return jnp.sqrt(values[:, 0] * values[:, 0] + values[:, 1] * values[:, 1])


def block_shards(total_shards, shard_rows):
    best = 1
    for factor in range(1, total_shards + 1):
        if total_shards % factor == 0 and factor * shard_rows <= BLOCK_LIMIT:
            best = factor
    return best


def fold_pairs(own, own_live, table, group, columns):

    def add_pieces(carry, piece, start):
        other, other_marks = piece
        shards = other.shape[2] // group
        per_block = block_shards(shards, group)
        width = per_block * group

        def one_block(number, total):
            first = number * width
            sub_spectra = lax.dynamic_slice_in_dim(other, first, width, 2)
            sub_live = lax.dynamic_slice_in_dim(other_marks, first, width, 2)[:, 0].astype(
                jnp.float32
            )
            block = correlate(own, own_live, sub_spectra, sub_live, table)
            block = block.reshape(
                block.shape[0], per_block, columns, group // columns, block.shape[2]
            )
            block = jnp.transpose(block, (0, 2, 1, 3, 4))
            block = block.reshape(block.shape[0], columns, width // columns, block.shape[4])
            slot = (start + first) // columns
            zero = jnp.zeros((), jnp.int32)
            return lax.dynamic_update_slice(
                total, block, (zero, zero, slot.astype(jnp.int32), zero)
            )

        return lax.fori_loop(0, shards // per_block, one_block, carry)

    return add_pieces


def per_device(spectra, masks):
    channels = spectra.shape[2]
    half_freq = spectra.shape[3]
    columns = lax.axis_size("col")
    column = lax.axis_index("col")
    partners = lax.axis_size("row") * channels
    live = masks.astype(jnp.float32)
    values = spectra.astype(jnp.float32)
    padded = with_halo(magnitudes(values), (("col", 2),), SMOOTH)
    whitened = whiten(values, padded, live)
    table = cosine_table(column * half_freq, half_freq)
    marks = live.astype(jnp.bfloat16)[:, None, :]
    adder = fold_pairs(whitened, live, table, channels, columns)
    empty = jnp.zeros((channels, columns, partners // columns, LAGS), jnp.float32)
    partial_sum = adder(
        empty,
        (
            lax.all_gather(whitened, "row", axis=2, tiled=True),
            lax.all_gather(marks, "row", axis=2, tiled=True),
        ),
        jnp.int32(0),
    )
    return lax.psum_scatter(partial_sum, "col", scatter_dimension=1, tiled=True)


def solution(mesh):
    placed = (P("hours", None, "row", "col"), P("hours", "row"))
    return jax.shard_map(
        per_device,
        mesh=mesh,
        in_specs=placed,
        out_specs=P(("hours", "row"), "col", None, None),
        check_vma=False,
    )
```

profile of v0, /device:TPU:0, one launch (start us, length us, event | category | flops | bytes accessed | tf_op | source)
XLA Modules:
  0.0 509.3 jit_solution(13442674106932536486)
XLA Ops:
  6.5 0.0 copy-start.1
  6.5 0.0 all-gather.3.cloned.1.call-start
  6.5 1.3 convert_element_type.552
  7.9 0.0 copy-start
  7.9 0.3 fusion.9
  8.1 0.1 fusion.60
  8.2 2.4 collective-permute-start
  10.6 1.3 collective-permute-start.1
  11.9 0.0 copy-done.1
  11.9 0.1 copy.5
  12.0 0.0 collective-permute-done
  12.0 1.7 collective-permute-done.1
  13.7 0.5 concatenate.7
  14.2 217.8 %reduce_window.7 = f32[12,8,2048]{2,1,0:T(8,128)S(1)} reduce-window(f32[12,8,2112]{2,1,0:T(8,128)S(1)} %concatenate.7, f32[]{:T(128)} %constant.50.clone.1), window={size=1x1x65}, to_apply=%region_0.0 | reduce-window | flops 12582912 | bytes 1597444 | tf_op jit(solution)/shard_map/reduce_window | solution.py:43
  231.9 0.1 multiply_add_fusion
  232.1 0.0 copy-done
  232.1 1.2 multiply_convert_fusion
  233.3 0.0 all-gather.3.cloned.1.call-update
  233.3 0.0 reduce-scatter.2.cloned.1.call-start
  233.3 27.7 %all-gather = bf16[12,64]{0,1:T(8,128)(2,1)S(1)} all-gather(bf16[12,8]{0,1:T(8,128)(2,1)S(1)} %get-tuple-element.81), channel_id=2, replica_groups=mesh['hours'=2,'row'=8,'col'=2] {'row'}, dimensions={1}, use_global_device_ids=true | all-gather | bytes 1728 | tf_op jit(solution)/shard_map/all_gather | solution.py:133
  261.0 0.1 convolution_maximum_fusion
  261.2 0.1 copy.6
  261.3 5.0 multiply_convert_fusion.2
  266.3 0.8 fusion.56
  267.2 1.2 fusion.57
  268.3 66.4 %all-gather.3.cloned.1.call-done = bf16[12,2,64,2048]{3,2,1,0:T(8,128)(2,1)} async-done(((bf16[12,2,8,2048]{3,2,1,0:T(8,128)(2,1)}), bf16[12,2,64,2048]{3,2,1,0:T(8,128)(2,1)}) %all-gather.3.cloned.1.call-update) | async-done | bytes 6291472 | tf_op jit(solution)/shard_map/all_gather | solution.py:132
  334.7 3.8 fusion.33
  338.5 1.6 fusion.32
  340.1 64.5 %add_add_fusion = f32[8,64,1,2048]{3,2,0,1:T(1,128)S(1)} fusion(f32[64,2048]{1,0:T(8,128)S(1)} %get-tuple-element.20, f32[8,2048]{1,0:T(8,128)S(1)} %get-tuple-element.54, f32[64,2048]{1,0:T(8,128)S(1)} %get-tuple-element.21, f32[8,2048]{1,0:T(8,128)S(1)} %get-tuple-element.55, f32[64,2048]{1,0:T(8,128)S(1)} %get-tuple-element.22, ...), kind=kLoop, calls=%fused_computation.3 | loop fusion | flops 49283072 | bytes 18350080 | tf_op jit(solution)/shard_map/while/body/eval_jaxpr/add | solution.py:59
  404.6 64.5 %subtract_add_fusion = f32[8,64,1,2048]{3,2,0,1:T(1,128)S(1)} fusion(f32[64,2048]{1,0:T(8,128)S(1)} %get-tuple-element.20, f32[8,2048]{1,0:T(8,128)S(1)} %get-tuple-element.54, f32[64,2048]{1,0:T(8,128)S(1)} %get-tuple-element.21, f32[8,2048]{1,0:T(8,128)S(1)} %get-tuple-element.55, f32[64,2048]{1,0:T(8,128)S(1)} %get-tuple-element.22, ...), kind=kLoop, calls=%fused_computation.2 | loop fusion | flops 49283072 | bytes 18350080 | tf_op jit(solution)/shard_map/while/body/eval_jaxpr/add | solution.py:60
  469.1 8.5 %pad_maximum_fusion = f32[8,64,2,2048]{3,2,0,1:T(2,128)} fusion(f32[8,64,1,2048]{3,2,0,1:T(1,128)S(1)} %subtract_add_fusion, f32[8,64,1,2048]{3,2,0,1:T(1,128)S(1)} %add_add_fusion), kind=kLoop, calls=%fused_computation | loop fusion | flops 2097152 | bytes 16777216 | tf_op jit(solution)/shard_map/while/body/eval_jaxpr/stack | solution.py:62
  477.6 11.8 %stack.11 = f32[8,8,2,4,4096]{4,0,3,2,1:T(8,128)} reshape(f32[8,64,2,2048]{3,2,0,1:T(2,128)} %pad_maximum_fusion) | data formatting | bytes 16777216 | tf_op jit(solution)/shard_map/while/body/eval_jaxpr/stack | solution.py:62
  489.4 4.7 fusion.1
  494.1 0.7 copy.8
  494.8 0.0 reduce-scatter.2.cloned.1.call-update
  494.8 6.0 %reduce-scatter.2.cloned.1.call-done = f32[8,1,32,128]{3,0,2,1:T(8,128)} async-done(((f32[8,2,32,128]{3,0,2,1:T(8,128)}), f32[8,1,32,128]{3,0,2,1:T(8,128)}) %reduce-scatter.2.cloned.1.call-update) | async-done | bytes 131088 | tf_op jit(solution)/shard_map/reduce_scatter | solution.py:137
  500.9 1.6 copy.9
  (3 shorter events, 0.0 us)
Async XLA Ops:
  6.5 5.3 %copy-start.1 = (s32[12,8]{0,1:T(8,128)S(1)}, s32[12,8]{0,1:T(8,128)}, u32[]{:S(2)}) copy-start(s32[12,8]{0,1:T(8,128)} %param.3) | copy-start | bytes 1156
  6.5 328.2 %all-gather.3.cloned.1.call-start = ((), (), s32[]{:S(2)}) async-start(), calls=%async_computation.1 | async-start | bytes 7077888 | tf_op jit(solution)/shard_map/all_gather | solution.py:132
  7.9 224.2 %copy-start = (bf16[12,2,8,2048]{3,2,1,0:T(8,128)(2,1)S(1)}, bf16[12,2,8,2048]{3,2,1,0:T(8,128)(2,1)}, u32[]{:S(2)}) copy-start(bf16[12,2,8,2048]{3,2,1,0:T(8,128)(2,1)} %param.2) | copy-start | bytes 2359300
  8.2 3.8 collective-permute-start
  10.6 3.1 collective-permute-start.1
  233.3 267.6 %reduce-scatter.2.cloned.1.call-start = ((), (), s32[]{:S(2)}) async-start(), calls=%async_computation.2 | async-start | bytes 393216 | tf_op jit(solution)/shard_map/reduce_scatter | solution.py:137
Sparse Core Ops, SparseCore 0:
  233.4 101.2 all-gather.2
  495.0 5.8 reduce-scatter.1
where the time goes:
time: 510 us; the launch traced here: 509 us
  other arithmetic  371 us (73%)
  waiting for transfers between devices  74.2 us (15%)
  blocking collectives  27.7 us (5%)
  local copies, waits for them, and re-layouts  14.8 us (3%)
  between operations  13.6 us (3%)
    another operation x1, other arithmetic, whiten(): lax.reduce_window(padded, jnp.array(0, padded.dtype), lax.add, (1, 1, 2 *...  218 us
    all_gather x1, waiting for transfers between devices, per_device(): lax.all_gather(whitened, 'row', axis=2, tiled=True)  66.4 us
    add x1, other arithmetic, stack_spectra(): imag = imag + (left_im * right_re - left_re * right_im)  64.5 us
    add x1, other arithmetic, stack_spectra(): real = real + (left_re * right_re + left_im * right_im)  64.5 us
    all_gather x1, blocking collectives, per_device(): lax.all_gather(marks, 'row', axis=2, tiled=True)  27.7 us
    another operation x1, local copies, waits for them, and re-layouts, stack_spectra(): jnp.stack([real, imag], axis=2) / count[:, :, None, None]  11.8 us
  transfers between devices with their start and end apart: 4, of which 3 were waited for; matrix products, arithmetic and copies ran while one was open for 1% of the time, Pallas kernels for 0%

commit v1 on v0

--- a/solution.py
+++ b/solution.py
@@ -9,6 +9,19 @@
 LAGS = 128
 EPSILON = 1e-05
 BLOCK_LIMIT = 64
+
+
+def ring_gather(x, axis, dim):
+    ways = lax.axis_size(axis)
+    up = [(d, (d + 1) % ways) for d in range(ways)]
+    down = [(d, (d - 1) % ways) for d in range(ways)]
+    earlier, later = ([x], [x])
+    for _ in range(ways // 2):
+        earlier.append(lax.ppermute(earlier[-1], axis, up))
+    for _ in range((ways - 1) // 2):
+        later.append(lax.ppermute(later[-1], axis, down))
+    line = jnp.concatenate([*earlier[::-1], *later[1:]], axis=dim)
+    return jnp.roll(line, (lax.axis_index(axis) - ways // 2) * x.shape[dim], axis=dim)
 
 
 def with_halo(cells, sides, width):
@@ -128,10 +141,7 @@
     empty = jnp.zeros((channels, columns, partners // columns, LAGS), jnp.float32)
     partial_sum = adder(
         empty,
-        (
-            lax.all_gather(whitened, "row", axis=2, tiled=True),
-            lax.all_gather(marks, "row", axis=2, tiled=True),
-        ),
+        (lax.all_gather(whitened, "row", axis=2, tiled=True), ring_gather(marks, "row", 2)),
         jnp.int32(0),
     )
     return lax.psum_scatter(partial_sum, "col", scatter_dimension=1, tiled=True)

time: 510 us -> 510 us (level)
  blocking collectives: 27.7 us -> 0 us
  starting transfers between devices: 3.69 us -> 18.8 us
  waiting for transfers between devices: 74.2 us -> 85.8 us
    all_gather x1 -> x0, blocking collectives: 27.7 us -> none  [per_device(): lax.all_gather(marks, 'row', axis=2, tiled=True)]
    ppermute x0 -> x7, starting transfers between devices: none -> 15.1 us  [the longest x3 12.7 us: ring_gather(): later.append(lax.ppermute(later[-1], axis, down))]
    ppermute x0 -> x7, waiting for transfers between devices: none -> 9.29 us  [the longest x4 9.28 us: ring_gather(): earlier.append(lax.ppermute(earlier[-1], axis, up))]
  transfers between devices with their start and end apart: 4 -> 11, of which waited for: 3 -> 6; matrix products, arithmetic and copies ran while one was open for 1% -> 2% of each run, Pallas kernels for 0% -> 0%
where the time goes in v1:
time: 510 us; the launch traced here: 509 us
  other arithmetic  371 us (73%)
  waiting for transfers between devices  85.8 us (17%)
  starting transfers between devices  18.8 us (4%)
  local copies, waits for them, and re-layouts  15.6 us (3%)
  between operations  13.6 us (3%)
    another operation x1, other arithmetic, whiten(): lax.reduce_window(padded, jnp.array(0, padded.dtype), lax.add, (1, 1, 2 *...  218 us
    all_gather x1, waiting for transfers between devices, per_device(): lax.all_gather(whitened, 'row', axis=2, tiled=True)  68.8 us
    add x1, other arithmetic, stack_spectra(): imag = imag + (left_im * right_re - left_re * right_im)  64.5 us
    add x1, other arithmetic, stack_spectra(): real = real + (left_re * right_re + left_im * right_im)  64.5 us
    ppermute x3, starting transfers between devices, ring_gather(): later.append(lax.ppermute(later[-1], axis, down))  12.7 us
    another operation x1, local copies, waits for them, and re-layouts, stack_spectra(): jnp.stack([real, imag], axis=2) / count[:, :, None, None]  11.8 us
  transfers between devices with their start and end apart: 11, of which 6 were waited for; matrix products, arithmetic and copies ran while one was open for 2% of the time, Pallas kernels for 0%

profile of v1, /device:TPU:0, one launch (start us, length us, event | category | flops | bytes accessed | tf_op | source)
XLA Modules:
  0.0 509.3 jit_solution(8398934782042140847)
XLA Ops:
  6.5 0.0 copy-start.1
  6.5 0.0 all-gather.2.cloned.1.call-start
  6.5 1.3 convert_element_type.552
  7.9 0.0 copy-start
  7.9 0.3 fusion.10
  8.1 0.1 fusion.64
  8.2 2.4 collective-permute-start
  10.6 1.3 collective-permute-start.1
  11.9 0.0 copy-done.1
  11.9 0.1 copy.10
  12.0 0.0 collective-permute-done
  12.0 1.7 collective-permute-done.1
  13.7 0.5 concatenate.13
  14.2 217.8 %reduce_window.7 = f32[12,8,2048]{2,1,0:T(8,128)S(1)} reduce-window(f32[12,8,2112]{2,1,0:T(8,128)S(1)} %concatenate.13, f32[]{:T(128)} %constant.74.clone.1), window={size=1x1x65}, to_apply=%region_0.0 | reduce-window | flops 12582912 | bytes 1597444 | tf_op jit(solution)/shard_map/reduce_window | solution.py:56
  231.9 0.1 multiply_add_fusion
  232.1 0.0 copy-done
  232.1 1.2 multiply_convert_fusion
  233.3 0.0 all-gather.2.cloned.1.call-update
  233.3 0.0 reduce-scatter.2.cloned.1.call-start
  233.3 2.4 collective-permute-start.2
  235.7 3.1 collective-permute-start.6
  238.9 0.1 copy.15
  238.9 5.0 multiply_convert_fusion.2
  244.0 0.0 collective-permute-done.2
  244.0 0.1 collective-permute-start.3
  244.1 0.1 copy.14
  244.1 0.0 collective-permute-done.6
  244.1 4.7 collective-permute-start.7
  248.9 0.1 copy.16
  248.9 1.5 collective-permute-done.3
  250.4 0.0 collective-permute-start.4
  250.4 0.1 copy.13
  250.5 0.0 collective-permute-done.7
  250.5 4.8 collective-permute-start.8
  255.4 0.1 copy.17
  255.4 1.5 collective-permute-done.4
  256.9 0.0 collective-permute-start.5
  256.9 0.1 copy.12
  257.0 0.0 collective-permute-done.8
  257.0 0.1 copy.18
  257.1 6.3 %collective-permute-done.5 = bf16[12,1,8]{0,2,1:T(8,128)(2,1)S(1)} collective-permute-done((bf16[12,1,8]{0,2,1:T(8,128)(2,1)S(1)}, bf16[12,1,8]{0,2,1:T(8,128)(2,1)S(1)}, u32[]{:S(2)}, u32[]{:S(2)}) %collective-permute-start.5) | collective-permute-done | bytes 224 | tf_op jit(solution)/shard_map/ppermute | solution.py:20
  263.4 0.1 copy.11
  263.5 0.1 concatenate.14
  263.6 0.2 fusion.2
  263.8 0.1 copy.27
  263.9 0.9 fusion.57
  264.8 1.2 fusion.58
  265.9 68.8 %all-gather.2.cloned.1.call-done = bf16[12,2,64,2048]{3,2,1,0:T(8,128)(2,1)} async-done(((bf16[12,2,8,2048]{3,2,1,0:T(8,128)(2,1)}), bf16[12,2,64,2048]{3,2,1,0:T(8,128)(2,1)}) %all-gather.2.cloned.1.call-update) | async-done | bytes 6291472 | tf_op jit(solution)/shard_map/all_gather | solution.py:144
  334.7 3.8 fusion.34
  338.5 1.6 fusion.33
  340.0 64.5 %add_add_fusion = f32[8,64,1,2048]{3,2,0,1:T(1,128)S(1)} fusion(f32[64,2048]{1,0:T(8,128)S(1)} %get-tuple-element.20, f32[8,2048]{1,0:T(8,128)S(1)} %get-tuple-element.54, f32[64,2048]{1,0:T(8,128)S(1)} %get-tuple-element.21, f32[8,2048]{1,0:T(8,128)S(1)} %get-tuple-element.55, f32[64,2048]{1,0:T(8,128)S(1)} %get-tuple-element.22, ...), kind=kLoop, calls=%fused_computation.3 | loop fusion | flops 49283072 | bytes 18350080 | tf_op jit(solution)/shard_map/while/body/eval_jaxpr/add | solution.py:72
  404.5 64.5 %subtract_add_fusion = f32[8,64,1,2048]{3,2,0,1:T(1,128)S(1)} fusion(f32[64,2048]{1,0:T(8,128)S(1)} %get-tuple-element.20, f32[8,2048]{1,0:T(8,128)S(1)} %get-tuple-element.54, f32[64,2048]{1,0:T(8,128)S(1)} %get-tuple-element.21, f32[8,2048]{1,0:T(8,128)S(1)} %get-tuple-element.55, f32[64,2048]{1,0:T(8,128)S(1)} %get-tuple-element.22, ...), kind=kLoop, calls=%fused_computation.2 | loop fusion | flops 49283072 | bytes 18350080 | tf_op jit(solution)/shard_map/while/body/eval_jaxpr/add | solution.py:73
  469.1 8.5 %pad_maximum_fusion = f32[8,64,2,2048]{3,2,0,1:T(2,128)} fusion(f32[8,64,1,2048]{3,2,0,1:T(1,128)S(1)} %subtract_add_fusion, f32[8,64,1,2048]{3,2,0,1:T(1,128)S(1)} %add_add_fusion), kind=kLoop, calls=%fused_computation | loop fusion | flops 2097152 | bytes 16777216 | tf_op jit(solution)/shard_map/while/body/eval_jaxpr/stack | solution.py:75
  477.6 11.8 %stack.11 = f32[8,8,2,4,4096]{4,0,3,2,1:T(8,128)} reshape(f32[8,64,2,2048]{3,2,0,1:T(2,128)} %pad_maximum_fusion) | data formatting | bytes 16777216 | tf_op jit(solution)/shard_map/while/body/eval_jaxpr/stack | solution.py:75
  489.4 4.7 fusion.1
  494.1 0.7 copy.28
  494.8 0.0 reduce-scatter.2.cloned.1.call-update
  494.8 6.0 %reduce-scatter.2.cloned.1.call-done = f32[8,1,32,128]{3,0,2,1:T(8,128)} async-done(((f32[8,2,32,128]{3,0,2,1:T(8,128)}), f32[8,1,32,128]{3,0,2,1:T(8,128)}) %reduce-scatter.2.cloned.1.call-update) | async-done | bytes 131088 | tf_op jit(solution)/shard_map/reduce_scatter | solution.py:147
  500.8 1.6 copy.29
  (3 shorter events, 0.0 us)
Async XLA Ops:
  6.5 5.3 %copy-start.1 = (s32[12,8]{0,1:T(8,128)S(1)}, s32[12,8]{0,1:T(8,128)}, u32[]{:S(2)}) copy-start(s32[12,8]{0,1:T(8,128)} %param.3) | copy-start | bytes 1156
  6.5 328.2 %all-gather.2.cloned.1.call-start = ((), (), s32[]{:S(2)}) async-start(), calls=%async_computation.1 | async-start | bytes 7077888 | tf_op jit(solution)/shard_map/all_gather | solution.py:144
  7.9 224.2 %copy-start = (bf16[12,2,8,2048]{3,2,1,0:T(8,128)(2,1)S(1)}, bf16[12,2,8,2048]{3,2,1,0:T(8,128)(2,1)}, u32[]{:S(2)}) copy-start(bf16[12,2,8,2048]{3,2,1,0:T(8,128)(2,1)} %param.2) | copy-start | bytes 2359300
  8.2 3.8 collective-permute-start
  10.6 3.1 collective-permute-start.1
  233.3 267.5 %reduce-scatter.2.cloned.1.call-start = ((), (), s32[]{:S(2)}) async-start(), calls=%async_computation.2 | async-start | bytes 393216 | tf_op jit(solution)/shard_map/reduce_scatter | solution.py:147
  233.3 10.6 %collective-permute-start.2 = (bf16[12,1,8]{0,2,1:T(8,128)(2,1)S(1)}, bf16[12,1,8]{0,2,1:T(8,128)(2,1)S(1)}, u32[]{:S(2)}, u32[]{:S(2)}) collective-permute-start(bf16[12,1,8]{0,2,1:T(8,128)(2,1)S(1)} %get-tuple-element.81), channel_id=1, source_target_pairs={{0,2},{2,4},{4,6},{6,8},{8,10},{10,12},{12,14},{14,0},{1,3},{3,5},... | collective-permute-start | bytes 584 | tf_op jit(solution)/shard_map/ppermute | solution.py:20
  235.7 8.4 %collective-permute-start.6 = (bf16[12,1,8]{0,2,1:T(8,128)(2,1)S(1)}, bf16[12,1,8]{0,2,1:T(8,128)(2,1)S(1)}, u32[]{:S(2)}, u32[]{:S(2)}) collective-permute-start(bf16[12,1,8]{0,2,1:T(8,128)(2,1)S(1)} %get-tuple-element.81), channel_id=1, source_target_pairs={{0,14},{2,0},{4,2},{6,4},{8,6},{10,8},{12,10},{14,12},{1,15},{3,1}... | collective-permute-start | bytes 584 | tf_op jit(solution)/shard_map/ppermute | solution.py:22
  244.0 6.4 %collective-permute-start.3 = (bf16[12,1,8]{0,2,1:T(8,128)(2,1)S(1)}, bf16[12,1,8]{0,2,1:T(8,128)(2,1)S(1)}, u32[]{:S(2)}, u32[]{:S(2)}) collective-permute-start(bf16[12,1,8]{0,2,1:T(8,128)(2,1)S(1)} %collective-permute-done.2), channel_id=1, source_target_pairs={{0,2},{2,4},{4,6},{6,8},{8,10},{10,12},{12,14},{14,0},{1,3},{3,5},... | collective-permute-start | bytes 584 | tf_op jit(solution)/shard_map/ppermute | solution.py:20
  244.1 6.4 %collective-permute-start.7 = (bf16[12,1,8]{0,2,1:T(8,128)(2,1)S(1)}, bf16[12,1,8]{0,2,1:T(8,128)(2,1)S(1)}, u32[]{:S(2)}, u32[]{:S(2)}) collective-permute-start(bf16[12,1,8]{0,2,1:T(8,128)(2,1)S(1)} %collective-permute-done.6), channel_id=1, source_target_pairs={{0,14},{2,0},{4,2},{6,4},{8,6},{10,8},{12,10},{14,12},{1,15},{3,1}... | collective-permute-start | bytes 584 | tf_op jit(solution)/shard_map/ppermute | solution.py:22
  250.4 6.5 %collective-permute-start.4 = (bf16[12,1,8]{0,2,1:T(8,128)(2,1)S(1)}, bf16[12,1,8]{0,2,1:T(8,128)(2,1)S(1)}, u32[]{:S(2)}, u32[]{:S(2)}) collective-permute-start(bf16[12,1,8]{0,2,1:T(8,128)(2,1)S(1)} %collective-permute-done.3), channel_id=1, source_target_pairs={{0,2},{2,4},{4,6},{6,8},{8,10},{10,12},{12,14},{14,0},{1,3},{3,5},... | collective-permute-start | bytes 584 | tf_op jit(solution)/shard_map/ppermute | solution.py:20
  250.5 6.5 %collective-permute-start.8 = (bf16[12,1,8]{0,2,1:T(8,128)(2,1)S(1)}, bf16[12,1,8]{0,2,1:T(8,128)(2,1)S(1)}, u32[]{:S(2)}, u32[]{:S(2)}) collective-permute-start(bf16[12,1,8]{0,2,1:T(8,128)(2,1)S(1)} %collective-permute-done.7), channel_id=1, source_target_pairs={{0,14},{2,0},{4,2},{6,4},{8,6},{10,8},{12,10},{14,12},{1,15},{3,1}... | collective-permute-start | bytes 584 | tf_op jit(solution)/shard_map/ppermute | solution.py:22
  256.9 6.5 %collective-permute-start.5 = (bf16[12,1,8]{0,2,1:T(8,128)(2,1)S(1)}, bf16[12,1,8]{0,2,1:T(8,128)(2,1)S(1)}, u32[]{:S(2)}, u32[]{:S(2)}) collective-permute-start(bf16[12,1,8]{0,2,1:T(8,128)(2,1)S(1)} %collective-permute-done.4), channel_id=1, source_target_pairs={{0,2},{2,4},{4,6},{6,8},{8,10},{10,12},{12,14},{14,0},{1,3},{3,5},... | collective-permute-start | bytes 584 | tf_op jit(solution)/shard_map/ppermute | solution.py:20
Sparse Core Ops, SparseCore 0:
  233.4 101.2 all-gather.1
  494.9 5.8 reduce-scatter.1
